TPU v7x, 256 devices: a whole 4x4x8 slice. The times are simulated.
256 devices in a mesh: ex: 8 (over z_lo, core), ey: 32 (over z_hi, x, y).
Axes of the slice: x: 4, y: 4, z: 8 (z_hi: 2, z_lo: 4; z = z_hi * 4 + z_lo), core: 2. Of those that a mesh axis runs over, the one named last changes fastest.
Arguments:
- tokens: bfloat16 [256, 256, 1024], P(('ex', 'ey')), may hold values from -16 to 16
- slot_param: bfloat16 [1024, 64], replicated, may hold values from -0.75 to 0.75
- weight_in: bfloat16 [64, 1024, 4096], P('ey', None, 'ex'), may hold values from -0.1875 to 0.1875
- weight_out: bfloat16 [64, 4096, 1024], P('ey', 'ex'), may hold values from -0.09375 to 0.09375
- grad_out: bfloat16 [256, 256, 1024], P(('ex', 'ey')), may hold values from -6 to 6
Outputs:
- grad_tokens: bfloat16 [256, 256, 1024], P(('ex', 'ey'))
- grad_param: float32 [1024, 64], replicated
- grad_win: bfloat16 [64, 1024, 4096], P('ey', None, 'ex')
- grad_wout: bfloat16 [64, 4096, 1024], P('ey', 'ex')
All inputs are finite; a program needn't handle non-finite values.
Results may differ from a plain program's by a relative error of at most 0.017.
Values may be sent and summed in bfloat16 or wider, within the bound.
A program may use at most 64 MiB of HBM per device.

v0:
```python
import jax
import jax.numpy as jnp
from jax import lax
from jax.sharding import Mesh
from jax.sharding import PartitionSpec as P

EX = ("ex_0", "ex_1")
EX_EY = ("ex_0", "ex_1", "ey")


def sum_in_order(tiles, axes, sequence):
    inside = tiles.shape[1:]
    tiles = tiles.reshape(*(lax.axis_size(a) for a in axes), *inside)
    tiles = jnp.moveaxis(tiles, sequence, range(len(axes))).reshape(-1, *inside)
    for k in sequence:
        tiles = lax.psum_scatter(tiles, axes[k], scatter_dimension=0, tiled=True)
    return tiles[0]


def in_blocks(array, dim, length):
    before, after = (array.shape[:dim], array.shape[dim + 1 :])
    return jnp.moveaxis(array.reshape(*before, length, -1, *after), dim, 0)


def summed_rows(array, axes, sequence, dim):
    length = lax.axis_size(axes)
    return sum_in_order(in_blocks(array, dim, length), axes, sequence)


def gelu_parts(pre):
    cdf = 0.5 * (1.0 + lax.erf(pre * 0.7071067811865476))
    slope = cdf + pre * jnp.exp(-0.5 * pre * pre) * 0.3989422804014327
    return (pre * cdf, slope)


def softmax_along(values, axis):
    top = jnp.max(values, axis=axis, keepdims=True)
    expo = jnp.exp(values - top)
    return expo / jnp.sum(expo, axis=axis, keepdims=True)


def route_in(stacked):
    moved = lax.all_to_all(stacked, "ey", split_axis=2, concat_axis=0, tiled=True)
    return lax.all_gather(moved, EX, axis=0, tiled=True)


def route_out(term_fn, total_rows):
    summed = summed_rows(
        term_fn(jnp.int32(0), total_rows // lax.axis_size(EX) * lax.axis_size(EX)).astype(
            jnp.bfloat16
        ),
        EX,
        (1, 0),
        0,
    ).astype(jnp.float32)
    return lax.all_to_all(
        summed.astype(jnp.bfloat16), "ey", split_axis=0, concat_axis=2, tiled=True
    )


def per_device(tokens, slot_param, weight_in, weight_out, grad_out):
    logits = jnp.einsum("ipd,ds->ips", tokens, slot_param, preferred_element_type=jnp.float32)
    dispatch = softmax_along(logits, 1)
    combine = softmax_along(logits, 2)
    dispatch_b = dispatch.astype(jnp.bfloat16)
    combine_b = combine.astype(jnp.bfloat16)
    slot_in = jnp.einsum(
        "ips,ipd->isd", dispatch_b, tokens, preferred_element_type=jnp.float32
    ).astype(jnp.bfloat16)
    slot_cot = jnp.einsum(
        "ips,ipd->isd", combine_b, grad_out, preferred_element_type=jnp.float32
    ).astype(jnp.bfloat16)
    arrived = route_in(jnp.stack((slot_in, slot_cot), axis=1))
    total_rows = arrived.shape[0]
    slot_x = arrived[:, 0]
    slot_g = arrived[:, 1]
    pre = jnp.einsum("red,edf->ref", slot_x, weight_in, preferred_element_type=jnp.float32)
    value, slope = gelu_parts(pre)
    hidden = value.astype(jnp.bfloat16)
    back = jnp.einsum("red,efd->ref", slot_g, weight_out, preferred_element_type=jnp.float32)
    dpre = (back * slope).astype(jnp.bfloat16)

    def paired_term(start, count):
        return jnp.concatenate(
            (
                jnp.einsum("ref,efd->red", hidden, weight_out, preferred_element_type=jnp.float32)[
                    :, None
                ],
                jnp.einsum("ref,edf->red", dpre, weight_in, preferred_element_type=jnp.float32)[
                    :, None
                ],
            ),
            axis=1,
        )

    paired = route_out(paired_term, total_rows)
    slot_out = paired[:, 0]
    grad_slot = paired[:, 1]
    grad_win = jnp.einsum("red,ref->edf", slot_x, dpre, preferred_element_type=jnp.float32).astype(
        jnp.bfloat16
    )
    grad_wout = jnp.einsum(
        "ref,red->efd", hidden, slot_g, preferred_element_type=jnp.float32
    ).astype(jnp.bfloat16)
    d_combine = jnp.einsum("ipd,isd->ips", grad_out, slot_out, preferred_element_type=jnp.float32)
    d_dispatch = jnp.einsum("ipd,isd->ips", tokens, grad_slot, preferred_element_type=jnp.float32)
    d_logits = dispatch * (d_dispatch - jnp.sum(dispatch * d_dispatch, axis=1, keepdims=True))
    d_logits = d_logits + combine * (
        d_combine - jnp.sum(combine * d_combine, axis=2, keepdims=True)
    )
    logit_grad = d_logits.astype(jnp.bfloat16)
    grad_tokens = jnp.einsum(
        "ips,isd->ipd", dispatch_b, grad_slot, preferred_element_type=jnp.float32
    )
    grad_tokens = grad_tokens + jnp.einsum(
        "ips,ds->ipd", logit_grad, slot_param, preferred_element_type=jnp.float32
    )
    local_param = jnp.einsum("ipd,ips->ds", tokens, logit_grad, preferred_element_type=jnp.float32)
    grad_param = lax.psum(local_param, EX_EY)
    return (grad_tokens.astype(jnp.bfloat16), grad_param, grad_win, grad_wout)


def solution(mesh):
    split = Mesh(mesh.devices.reshape(4, 2, mesh.shape["ey"]), ("ex_0", "ex_1", "ey"))
    return jax.shard_map(
        per_device,
        mesh=split,
        in_specs=(
            P(EX_EY, None, None),
            P(),
            P("ey", None, EX),
            P("ey", EX, None),
            P(EX_EY, None, None),
        ),
        out_specs=(P(EX_EY, None, None), P(), P("ey", None, EX), P("ey", EX, None)),
        check_vma=False,
    )
```

profile of v0, /device:TPU:1, one launch (start us, length us, event | category | flops | bytes accessed | tf_op | source)
XLA Modules:
  0.0 418.0 jit_solution(196067309297569867)
XLA Ops:
  7.2 0.0 copy-start
  7.2 0.0 all-gather.3.cloned.1.call-start
  7.2 1.6 fusion.34
  8.8 0.2 fusion.23
  9.0 1.3 fusion.4
  10.3 1.2 fusion.5
  11.6 0.3 copy.31
  11.9 26.3 %all_to_all.36 = bf16[1,2,64,1024]{3,1,0,2:T(2,128)(2,1)S(1)} all-to-all(bf16[1,2,64,1024]{3,1,0,2:T(2,128)(2,1)S(1)} %copy.31), channel_id=1, replica_groups=mesh['ex_0'=4,'ex_1'=2,'ey'=32] {'ey'}, dimensions={2} | all-to-all | bytes 524288 | tf_op jit(solution)/shard_map/all_to_all | solution.py:43
  38.2 0.8 copy.59
  39.0 0.0 all-gather.3.cloned.1.call-update
  39.0 0.0 reduce-scatter.3.cloned.1.call-start
  39.1 35.4 %all-gather.3.cloned.1.call-done = bf16[256,1,2,2,1024]{4,0,3,2,1:T(8,128)(2,1)} async-done(((bf16[32,1,2,2,1024]{4,0,3,2,1:T(8,128)(2,1)}), bf16[256,1,2,2,1024]{4,0,3,2,1:T(8,128)(2,1)}) %all-gather.3.cloned.1.call-update) | async-done | bytes 2097168 | tf_op jit(solution)/shard_map/all_gather | solution.py:44
  74.5 2.8 convolution_bitcast_fusion.1
  77.3 0.0 copy-done
  77.3 0.0 copy-done.3
  77.3 1.0 fusion.2
  78.3 0.0 copy-start.5
  78.3 0.0 copy-start.1
  78.3 0.7 convolution_convert_fusion.3
  79.1 1.0 copy-done.1
  80.1 0.7 convolution_convert_fusion.2
  80.9 0.0 copy-done.5
  80.9 0.2 pad_maximum_fusion
  81.1 1.5 copy.41
  82.6 0.0 reduce-scatter.3.cloned.1.call-update
  82.6 0.0 reduce-scatter.5.cloned.1.call-start
  82.6 16.7 %reduce-scatter.3.cloned.1.call-done = bf16[4,32,2,2,1024]{4,1,3,2,0:T(8,128)(2,1)} async-done(((bf16[8,32,2,2,1024]{4,1,3,2,0:T(8,128)(2,1)}), bf16[4,32,2,2,1024]{4,1,3,2,0:T(8,128)(2,1)}) %reduce-scatter.3.cloned.1.call-update) | async-done | bytes 1048592 | tf_op jit(solution)/shard_map/reduce_scatter | solution.py:16
  99.4 0.0 reduce-scatter.5.cloned.1.call-update
  99.4 35.7 %reduce-scatter.5.cloned.1.call-done = bf16[1,32,2,2,1024]{4,1,3,2,0:T(8,128)(2,1)} async-done(((bf16[4,32,2,2,1024]{4,1,3,2,0:T(8,128)(2,1)}), bf16[1,32,2,2,1024]{4,1,3,2,0:T(8,128)(2,1)}) %reduce-scatter.5.cloned.1.call-update) | async-done | bytes 262160 | tf_op jit(solution)/shard_map/reduce_scatter | solution.py:16
  135.1 1.9 copy.35
  137.0 9.6 %all-to-all-start.1 = ((bf16[32,2,2,1024]{3,2,1,0:T(2,128)(2,1)}), bf16[32,2,2,1024]{3,2,1,0:T(2,128)(2,1)S(1)}, u32[]{:S(2)}, u32[]{:S(2)}) async-start(bf16[32,2,2,1024]{3,2,1,0:T(2,128)(2,1)} %copy.35), calls=%async_computation.3 | async-start | bytes 524288 | tf_op jit(solution)/shard_map/all_to_all | solution.py:56
  146.6 0.0 all-reduce.2.cloned.1.call-start
  146.7 0.0 copy-start.4
  146.7 3.6 convolution_convert_fusion.1
  150.3 0.0 copy-done.4
  150.3 2.1 convolution_convert_fusion
  152.4 6.3 %all-to-all-done.1 = bf16[32,2,2,1024]{3,2,1,0:T(2,128)(2,1)S(1)} async-done(((bf16[32,2,2,1024]{3,2,1,0:T(2,128)(2,1)}), bf16[32,2,2,1024]{3,2,1,0:T(2,128)(2,1)S(1)}, u32[]{:S(2)}, u32[]{:S(2)}) %all-to-all-start.1) | async-done | bytes 262176 | tf_op jit(solution)/shard_map/all_to_all | solution.py:56
  158.7 0.2 copy.36
  158.9 0.4 fusion.35
  159.2 0.0 copy-start.6
  159.2 1.4 convolution_bitcast_fusion.3
  160.6 1.4 fusion.20
  162.0 0.4 multiply_reduce_fusion.1
  162.4 1.0 convolution_bitcast_fusion.2
  163.4 0.0 all-reduce.2.cloned.1.call-update
  163.4 2.4 fusion.3
  165.8 243.9 %all-reduce.2.cloned.1.call-done = f32[1024,64]{0,1:T(8,128)} async-done(((f32[1024,64]{0,1:T(8,128)}), f32[1024,64]{0,1:T(8,128)}) %all-reduce.2.cloned.1.call-update) | async-done | bytes 262160 | tf_op jit(solution)/shard_map/psum | solution.py:119
  409.7 1.7 copy.61
  (5 shorter events, 0.0 us)
Async XLA Ops:
  7.2 70.1 %copy-start = (bf16[2,512,1024]{2,1,0:T(8,128)(2,1)S(1)}, bf16[2,512,1024]{2,1,0:T(8,128)(2,1)}, u32[]{:S(2)}) copy-start(bf16[2,512,1024]{2,1,0:T(8,128)(2,1)} %param.8) | copy-start | bytes 6291460
  7.2 67.4 %all-gather.3.cloned.1.call-start = ((), (), s32[]{:S(2)}) async-start(), calls=%async_computation.7 | async-start | bytes 2359296 | tf_op jit(solution)/shard_map/all_gather | solution.py:44
  39.0 60.3 %reduce-scatter.3.cloned.1.call-start = ((), (), s32[]{:S(2)}) async-start(), calls=%async_computation.4 | async-start | bytes 3145728 | tf_op jit(solution)/shard_map/reduce_scatter | solution.py:16
  74.5 2.8 copy-start.3
  78.3 2.5 copy-start.5
  78.3 1.8 copy-start.1
  82.6 52.5 %reduce-scatter.5.cloned.1.call-start = ((), (), s32[]{:S(2)}) async-start(), calls=%async_computation.5 | async-start | bytes 1310720 | tf_op jit(solution)/shard_map/reduce_scatter | solution.py:16
  137.0 21.7 %all-to-all-start.1 = ((bf16[32,2,2,1024]{3,2,1,0:T(2,128)(2,1)}), bf16[32,2,2,1024]{3,2,1,0:T(2,128)(2,1)S(1)}, u32[]{:S(2)}, u32[]{:S(2)}) async-start(bf16[32,2,2,1024]{3,2,1,0:T(2,128)(2,1)} %copy.35), calls=%async_computation.3 | async-start | bytes 524288 | tf_op jit(solution)/shard_map/all_to_all | solution.py:56
  146.6 263.1 %all-reduce.2.cloned.1.call-start = ((), (), s32[]{:S(2)}) async-start(), calls=%async_computation.6 | async-start | bytes 524288 | tf_op jit(solution)/shard_map/psum | solution.py:119
  146.7 3.6 copy-start.4
  152.4 9.6 %copy-start.2 = (bf16[1,256,1024]{2,1,0:T(8,128)(2,1)S(1)}, bf16[1,256,1024]{2,1,0:T(8,128)(2,1)}, u32[]{:S(2)}) copy-start(bf16[1,256,1024]{2,1,0:T(8,128)(2,1)} %param.5) | copy-start | bytes 1572868
  159.2 4.2 copy-start.6
Sparse Core Ops, SparseCore 0:
  39.2 35.3 all-gather.2
  82.7 16.6 reduce-scatter.2
  102.1 32.9 reduce-scatter.4
  163.5 246.1 all-reduce.1
where the time goes:
time: 419 us; the launch traced here: 418 us
  waiting for transfers between devices  338 us (81%)
  blocking collectives  26.3 us (6%)
  matrix products  21.6 us (5%)
  between operations  13.9 us (3%)
  starting transfers between devices  9.79 us (2%)
  local copies, waits for them, and re-layouts  7.79 us (2%)
    psum x1, waiting for transfers between devices, per_device(): grad_param = lax.psum(local_param, EX_EY)  244 us
    reduce_scatter x2, waiting for transfers between devices, sum_in_order(): tiles = lax.psum_scatter(tiles, axes[k], scatter_dimension=0, tiled=True)  52.4 us
    all_gather x1, waiting for transfers between devices, route_in(): return lax.all_gather(moved, EX, axis=0, tiled=True)  35.4 us
    all_to_all x1, blocking collectives, route_in(): lax.all_to_all(stacked, 'ey', split_axis=2, concat_axis=0, tiled=True)  26.3 us
    all_to_all x1, starting transfers between devices, route_out(): lax.all_to_all(summed.astype(jnp.bfloat16), 'ey', split_axis=0, concat_ax...  9.63 us
  transfers between devices with their start and end apart: 5, of which 5 were waited for; matrix products, arithmetic and copies ran while one was open for 2% of the time, Pallas kernels for 0%

commit v1 on v0

v1 whole, which is shorter than its diff:
```python
import functools

import jax
import jax.numpy as jnp
from jax import lax
from jax.experimental import pallas as pl
from jax.experimental.pallas import tpu as pltpu
from jax.sharding import Mesh
from jax.sharding import PartitionSpec as P

AXES = ("zl", "core", "zh", "xy")
EX = ("zl", "core")
EY = ("zh", "xy")
ALL = AXES
ZH = 2
LANES = 128
F32 = jnp.float32
BF16 = jnp.bfloat16


def dot(a, b, ca, cb):
    return lax.dot_general(a, b, (((ca,), (cb,)), ((), ())), preferred_element_type=F32)


def softmax_along(values, axis):
    top = jnp.max(values, axis=axis, keepdims=True)
    expo = jnp.exp(values - top)
    return expo / jnp.sum(expo, axis=axis, keepdims=True)


def gelu_parts(pre):
    cdf = 0.5 * (1.0 + lax.erf(pre * 0.7071067811865476))
    slope = cdf + pre * jnp.exp(-0.5 * pre * pre) * 0.3989422804014327
    return (pre * cdf, slope)


def kernel(
    ZL, XY,
    tok_hbm, par_hbm, wi_hbm, wo_hbm, go_hbm,
    gt_hbm, gp_hbm, gwi_hbm, gwo_hbm,
    tok, par, go, wi, wo,
    disp, comb, disp_b, comb_b,
    rows32, send1, recv1, planes, gathered,
    pre_s, back_s, hid, dpre,
    ysend, yrecv, send2, recv2, slots,
    gt_v, gwi_v, gwo_v,
    xsend, xrecv, zsend, zrecv, usend, urecv, gp_v,
    in_sem, out_sem, w_send, w_recv, g_send, g_recv,
    a_send, a_recv, b_send, b_recv, y_send, y_recv, c_send, c_recv,
    x_send, x_recv, z_send, z_recv, u_send, u_recv,
):
    T = 2 * XY
    NZ = ZL * ZH
    D = tok.shape[1]
    J = D // LANES
    PAIR = 2 * J
    zl = lax.axis_index("zl")
    core = lax.axis_index("core")
    zh = lax.axis_index("zh")
    xy = lax.axis_index("xy")
    me_t = xy * 2 + core
    me_z = zh * ZL + zl

    def in_plane(d):
        t = lax.rem(me_t + d, T)
        return t, (zl, lax.rem(t, 2), zh, lax.div(t, 2))

    def along_z(d):
        z = lax.rem(me_z + d, NZ)
        return z, (lax.rem(z, ZL), core, lax.div(z, ZL), xy)

    sibling = (zl, 1 - core, zh, xy)

    def remote(src, dst, send_sem, recv_sem, device):
        return pltpu.make_async_remote_copy(
            src_ref=src, dst_ref=dst, send_sem=send_sem, recv_sem=recv_sem,
            device_id=device, device_id_type=pl.DeviceIdType.MESH,
        )

    barrier = pltpu.get_barrier_semaphore()

    def greet_plane(d, carry):
        pl.semaphore_signal(barrier, inc=1, device_id=in_plane(d)[1], device_id_type=pl.DeviceIdType.MESH)
        return carry

    def greet_z(d, carry):
        pl.semaphore_signal(barrier, inc=1, device_id=along_z(d)[1], device_id_type=pl.DeviceIdType.MESH)
        return carry

    loads = [
        pltpu.make_async_copy(tok_hbm, tok, in_sem.at[0]),
        pltpu.make_async_copy(par_hbm, par, in_sem.at[1]),
        pltpu.make_async_copy(go_hbm, go, in_sem.at[2]),
        pltpu.make_async_copy(wi_hbm.at[core], wi.at[core], in_sem.at[3]),
        pltpu.make_async_copy(wo_hbm.at[core], wo.at[core], in_sem.at[4]),
    ]
    for load in loads:
        load.start()
    lax.fori_loop(1, T, greet_plane, 0)
    lax.fori_loop(1, NZ, greet_z, 0)

    def pack(part, h, w):
        for j in range(J):
            rows32[pl.ds(h * PAIR + w * J + j, T, stride=ZH * PAIR), :] = part[:, j * LANES : (j + 1) * LANES]

    def unpack(h, w, j):
        return rows32[pl.ds(h * PAIR + w * J + j, T, stride=ZH * PAIR), :].astype(BF16)

    def all_to_all(send, recv, send_sem, recv_sem):
        def go_to(d, carry):
            t, device = in_plane(d)
            remote(send.at[t], recv.at[me_t], send_sem, recv_sem, device).start()
            return carry

        lax.fori_loop(1, T, go_to, 0)

    def wait_all(ref, count, sem):
        part = ref.at[pl.ds(0, count)]
        pltpu.make_async_copy(part, part, sem).wait()

    loads[0].wait()
    loads[1].wait()
    logits = dot(tok[...], par[...], 1, 0)
    dispatch = softmax_along(logits, 0)
    combine = softmax_along(logits, 1)
    disp[...] = dispatch
    comb[...] = combine
    disp_b[...] = dispatch.astype(BF16)
    comb_b[...] = combine.astype(BF16)
    slot_in = dot(disp_b[...], tok[...], 0, 0)
    for h in range(ZH):
        pack(slot_in[h * T : (h + 1) * T], h, 0)
    loads[2].wait()
    slot_cot = dot(comb_b[...], go[...], 0, 0)
    for h in range(ZH):
        pack(slot_cot[h * T : (h + 1) * T], h, 1)
    send1[...] = rows32[...].astype(BF16).reshape(send1.shape)

    pl.semaphore_wait(barrier, T - 1 + NZ - 1)
    all_to_all(send1, recv1, a_send, a_recv)
    swap = [
        remote(wi_hbm.at[1 - core], wi.at[core], w_send.at[0], w_recv.at[0], sibling),
        remote(wo_hbm.at[1 - core], wo.at[core], w_send.at[1], w_recv.at[1], sibling),
    ]
    for copy in swap:
        copy.start()
    wait_all(send1, T - 1, a_send)
    wait_all(recv1, T - 1, a_recv)
    recv1[me_t] = send1[me_t]
    rows32[...] = recv1[...].reshape(rows32.shape).astype(F32)
    for h in range(ZH):
        for w in range(2):
            for j in range(J):
                planes[h, w, :, j * LANES : (j + 1) * LANES] = unpack(h, w, j)

    def send_plane(d, carry):
        z, device = along_z(d)
        remote(planes.at[lax.div(z, ZL)], gathered.at[me_z], b_send.at[z], b_recv.at[me_z], device).start()
        return carry

    def wait_plane(d, carry):
        z, device = along_z(d)
        remote(planes.at[0], gathered.at[z], b_send.at[z], b_recv.at[z], device).wait()
        return carry

    lax.fori_loop(1, NZ, send_plane, 0)
    gathered[me_z] = planes[zh]
    for copy in loads[3:] + swap:
        copy.wait()
    lax.fori_loop(1, NZ, wait_plane, 0)

    rows = NZ * T
    slot_x = gathered[:, 0].reshape(rows, D)
    slot_g = gathered[:, 1].reshape(rows, D)
    step = min(16, rows)
    for f in range(2):
        pre_s[...] = dot(slot_x, wi[f], 1, 0)
        back_s[...] = dot(slot_g, wo[f], 1, 1)

        def activate(k, carry):
            part = pl.ds(pl.multiple_of(k * step, step), step)
            value, slope = gelu_parts(pre_s[part, :])
            hid[f, part, :] = value.astype(BF16)
            dpre[f, part, :] = (back_s[part, :] * slope).astype(BF16)
            return carry

        lax.fori_loop(0, rows // step, activate, 0)
    ysend[:, 0] = (dot(hid[0], wo[0], 1, 0) + dot(hid[1], wo[1], 1, 0)).astype(BF16).reshape(NZ, T, D)
    ysend[:, 1] = (dot(dpre[0], wi[0], 1, 1) + dot(dpre[1], wi[1], 1, 1)).astype(BF16).reshape(NZ, T, D)

    def send_back(d, carry):
        z, device = along_z(d)
        remote(ysend.at[z], yrecv.at[me_z], y_send.at[z], y_recv.at[me_z], device).start()
        return carry

    def wait_back(d, carry):
        z, device = along_z(d)
        remote(ysend.at[z], yrecv.at[z], y_send.at[z], y_recv.at[z], device).wait()
        return carry

    lax.fori_loop(1, NZ, send_back, 0)
    yrecv[me_z] = ysend[me_z]
    for f in range(2):
        gwi_v[f] = dot(slot_x, dpre[f], 0, 0).astype(BF16)
        gwo_v[f] = dot(hid[f], slot_g, 0, 0).astype(BF16)
    stores = [
        pltpu.make_async_copy(gwi_v.at[core], gwi_hbm.at[core], out_sem.at[0]),
        pltpu.make_async_copy(gwo_v.at[core], gwo_hbm.at[core], out_sem.at[1]),
        remote(gwi_v.at[1 - core], gwi_hbm.at[core], g_send.at[0], g_recv.at[0], sibling),
        remote(gwo_v.at[1 - core], gwo_hbm.at[core], g_send.at[1], g_recv.at[1], sibling),
    ]
    for copy in stores:
        copy.start()
    lax.fori_loop(1, NZ, wait_back, 0)
    for h in range(ZH):
        for w in range(2):
            total = yrecv[h * ZL, w].astype(F32)
            for k in range(1, ZL):
                total = total + yrecv[h * ZL + k, w].astype(F32)
            pack(total, h, w)
    send2[...] = rows32[...].astype(BF16).reshape(send2.shape)
    all_to_all(send2, recv2, c_send, c_recv)
    wait_all(send2, T - 1, c_send)
    wait_all(recv2, T - 1, c_recv)
    recv2[me_t] = send2[me_t]
    rows32[...] = recv2[...].reshape(rows32.shape).astype(F32)
    for h in range(ZH):
        for w in range(2):
            for j in range(J):
                slots[w, h * T : (h + 1) * T, j * LANES : (j + 1) * LANES] = unpack(h, w, j)

    d_combine = dot(go[...], slots[0], 1, 1)
    d_dispatch = dot(tok[...], slots[1], 1, 1)
    dispatch = disp[...]
    combine = comb[...]
    d_logits = dispatch * (d_dispatch - jnp.sum(dispatch * d_dispatch, axis=0, keepdims=True))
    d_logits = d_logits + combine * (d_combine - jnp.sum(combine * d_combine, axis=1, keepdims=True))
    logit_grad = d_logits.astype(BF16)
    local_param = dot(logit_grad, tok[...], 0, 0)

    S = disp.shape[1]
    for r in range(S // 8):
        for j in range(J):
            k = r * J + j
            xsend[k // 2, k % 2] = local_param[r * 8 : (r + 1) * 8, j * LANES : (j + 1) * LANES]
    all_to_all(xsend, xrecv, x_send, x_recv)
    gt_v[...] = (dot(disp_b[...], slots[1], 1, 0) + dot(logit_grad, par[...], 1, 1)).astype(BF16)
    store_gt = pltpu.make_async_copy(gt_v, gt_hbm, out_sem.at[2])
    store_gt.start()
    wait_all(xsend, T - 1, x_send)
    wait_all(xrecv, T - 1, x_recv)
    xrecv[me_t] = xsend[me_t]
    zsend[...] = jnp.sum(xrecv[...], axis=0)

    def send_sum(d, carry):
        z, device = along_z(d)
        remote(zsend, zrecv.at[me_z], z_send, z_recv, device).start()
        return carry

    lax.fori_loop(1, NZ, send_sum, 0)
    wait_all(zrecv, NZ - 1, z_send)
    wait_all(zrecv, NZ - 1, z_recv)
    zrecv[me_z] = zsend[...]
    usend[...] = jnp.sum(zrecv[...], axis=0)

    def send_total(d, carry):
        remote(usend, urecv.at[me_t], u_send, u_recv, in_plane(d)[1]).start()
        return carry

    lax.fori_loop(1, T, send_total, 0)
    wait_all(urecv, T - 1, u_send)
    wait_all(urecv, T - 1, u_recv)
    urecv[me_t] = usend[...]
    for r in range(S // 8):
        for j in range(J):
            k = r * J + j
            gp_v[r * 8 : (r + 1) * 8, j * LANES : (j + 1) * LANES] = urecv[k // 2, k % 2]
    store_gp = pltpu.make_async_copy(gp_v, gp_hbm, out_sem.at[3])
    store_gp.start()
    for copy in stores + [store_gt, store_gp]:
        copy.wait()


def per_device(ZL, XY, tokens, slot_param, weight_in, weight_out, grad_out):
    _, patches, D = tokens.shape
    S = slot_param.shape[1]
    F = weight_in.shape[2]
    T = 2 * XY
    NZ = ZL * ZH
    rows = NZ * T
    PAIR = 2 * (D // LANES)
    DMA = pltpu.SemaphoreType.DMA
    anywhere = pl.BlockSpec(memory_space=pl.ANY)
    vmem = pltpu.VMEM
    scratch = [
        vmem((patches, D), BF16), vmem((D, S), BF16), vmem((patches, D), BF16),
        vmem((2, D, F), BF16), vmem((2, F, D), BF16),
        vmem((patches, S), F32), vmem((patches, S), F32), vmem((patches, S), BF16), vmem((patches, S), BF16),
        vmem((T * ZH * PAIR, LANES), F32),
        vmem((T, ZH * PAIR, LANES), BF16), vmem((T, ZH * PAIR, LANES), BF16),
        vmem((ZH, 2, T, D), BF16), vmem((NZ, 2, T, D), BF16),
        vmem((rows, F), F32), vmem((rows, F), F32), vmem((2, rows, F), BF16), vmem((2, rows, F), BF16),
        vmem((NZ, 2, T, D), BF16), vmem((NZ, 2, T, D), BF16),
        vmem((T, ZH * PAIR, LANES), BF16), vmem((T, ZH * PAIR, LANES), BF16),
        vmem((2, S, D), BF16),
        vmem((patches, D), BF16), vmem((2, D, F), BF16), vmem((2, F, D), BF16),
        vmem((T, 2, 8, LANES), F32), vmem((T, 2, 8, LANES), F32),
        vmem((2, 8, LANES), F32), vmem((NZ, 2, 8, LANES), F32),
        vmem((2, 8, LANES), F32), vmem((T, 2, 8, LANES), F32), vmem((S, D), F32),
        DMA((5,)), DMA((4,)), DMA((2,)), DMA((2,)), DMA((2,)), DMA((2,)),
        DMA, DMA, DMA((NZ,)), DMA((NZ,)), DMA((NZ,)), DMA((NZ,)), DMA, DMA,
        DMA, DMA, DMA, DMA, DMA, DMA,
    ]
    grad_tokens, grad_param, grad_win, grad_wout = pl.pallas_call(
        functools.partial(kernel, ZL, XY),
        out_shape=(
            jax.ShapeDtypeStruct((patches, D), BF16),
            jax.ShapeDtypeStruct((S, D), F32),
            jax.ShapeDtypeStruct(weight_in.shape, BF16),
            jax.ShapeDtypeStruct(weight_out.shape, BF16),
        ),
        in_specs=[anywhere] * 5,
        out_specs=[anywhere] * 4,
        scratch_shapes=scratch,
        compiler_params=pltpu.CompilerParams(
            collective_id=0, has_side_effects=True, vmem_limit_bytes=48 * 1024 * 1024
        ),
    )(tokens[0], slot_param, weight_in, weight_out, grad_out[0])
    return grad_tokens[None], grad_param.T, grad_win, grad_wout


def solution(mesh):
    ZL = mesh.shape["ex"] // 2
    XY = mesh.shape["ey"] // ZH
    split = Mesh(mesh.devices.reshape(ZL, 2, ZH, XY), AXES)
    return jax.shard_map(
        functools.partial(per_device, ZL, XY),
        mesh=split,
        in_specs=(P(ALL, None, None), P(), P(EY, None, EX), P(EY, EX, None), P(ALL, None, None)),
        out_specs=(P(ALL, None, None), P(), P(EY, None, EX), P(EY, EX, None)),
        check_vma=False,
    )
```

time: 419 us -> 106 us (0.25)
  waiting for transfers between devices: 338 us -> 0 us
  Pallas kernels: 0 us -> 96.6 us
  blocking collectives: 26.3 us -> 0 us
  matrix products: 21.6 us -> 0 us
  between operations: 13.9 us -> 0.66 us
  starting transfers between devices: 9.79 us -> 0 us
    psum x1 -> x0, waiting for transfers between devices: 244 us -> none  [per_device(): grad_param = lax.psum(local_param, EX_EY)]
    pallas_call x0 -> x1, Pallas kernels: none -> 96.6 us  [per_device(): pl.pallas_call(functools.partial(kernel, ZL, XY), out_shape=(jax.ShapeDty...]
    reduce_scatter x2 -> x0, waiting for transfers between devices: 52.4 us -> none  [sum_in_order(): tiles = lax.psum_scatter(tiles, axes[k], scatter_dimension=0, tiled=True)]
    all_gather x1 -> x0, waiting for transfers between devices: 35.4 us -> none  [route_in(): return lax.all_gather(moved, EX, axis=0, tiled=True)]
    all_to_all x1 -> x0, blocking collectives: 26.3 us -> none  [route_in(): lax.all_to_all(stacked, 'ey', split_axis=2, concat_axis=0, tiled=True)]
    dot_general x14 -> x0, matrix products: 21.6 us -> none  [the longest x1 3.58 us: per_device(): jnp.einsum('red,ref->edf', slot_x, dpre, preferred_element_type=jnp.float32)]
    all_to_all x1 -> x0, starting transfers between devices: 9.63 us -> none  [route_out(): lax.all_to_all(summed.astype(jnp.bfloat16), 'ey', split_axis=0, concat_ax...]
    all_to_all x1 -> x0, waiting for transfers between devices: 6.28 us -> none  [route_out(): lax.all_to_all(summed.astype(jnp.bfloat16), 'ey', split_axis=0, concat_ax...]
  transfers between devices with their start and end apart: 5 -> 0, of which waited for: 5 -> 0; matrix products, arithmetic and copies ran while one was open for 2% -> 0% of each run, Pallas kernels for 0% -> 0%
where the time goes in v1:
time: 106 us
  Pallas kernels  96.6 us (91%)
  local copies, waits for them, and re-layouts  8.32 us (8%)
    pallas_call x1, Pallas kernels, per_device(): pl.pallas_call(functools.partial(kernel, ZL, XY), out_shape=(jax.ShapeDty...  96.6 us
    unnamed x11, local copies, waits for them, and re-layouts  8.32 us

profile of v1, /device:TPU:1, one launch (start us, length us, event | category | flops | bytes accessed | tf_op | source)
XLA Modules:
  0.0 105.6 jit_solution(10317858287487230874)
XLA Ops:
  0.6 1.1 %copy.9.par_hbm = bf16[1024,64]{1,0:T(8,128)(2,1)S(1)} copy(bf16[1024,64]{0,1:T(8,128)(2,1)} %param.6) | data formatting | bytes 262144 | tf_op args[1]
  1.7 0.0 copy-start
  1.7 1.0 copy-done
  2.8 0.0 copy-start.1
  2.8 1.0 copy-done.1
  3.8 96.6 %shard_map.84 = (bf16[256,1024]{1,0:T(8,128)(2,1)S(1)}, f32[64,1024]{1,0:T(8,128)S(1)}, bf16[2,1024,512]{2,1,0:T(8,128)(2,1)S(1)}, bf16[2,512,1024]{2,1,0:T(8,128)(2,1)}) custom-call(bf16[256,1024]{1,0:T(8,128)(2,1)S(1)} %bitcast.5, bf16[1024,64]{1,0:T(8,128)(2,1)S(1)} %copy.9.par_hbm, bf16[2,1024,512]{2,1,0:T(8,128)(2,1)} %wi_hbm.1, ...), custom_call_target="tpu_custom_call" | custom-call | tf_op jit(solution)/shard_map/pallas_call | solution.py:314
  100.4 0.8 copy.14
  101.2 0.7 copy.15
  101.9 0.0 copy-start.2
  101.9 1.3 %copy.16 = bf16[2,1024,512]{2,1,0:T(8,128)(2,1)} copy(bf16[2,1024,512]{2,1,0:T(8,128)(2,1)S(1)} %get-tuple-element.18) | data formatting | bytes 4194304
  103.3 1.0 copy-done.2
  104.3 1.3 %copy.17 = bf16[2,512,1024]{2,1,0:T(8,128)(2,1)} copy(bf16[2,512,1024]{2,1,0:T(8,128)(2,1)S(1)} %copy-done.2) | data formatting | bytes 4194304
Async XLA Ops:
  1.7 1.0 copy-start
  2.8 1.0 copy-start.1
  101.9 2.3 %copy-start.2 = (bf16[2,512,1024]{2,1,0:T(8,128)(2,1)S(1)}, bf16[2,512,1024]{2,1,0:T(8,128)(2,1)}, u32[]{:S(2)}) copy-start(bf16[2,512,1024]{2,1,0:T(8,128)(2,1)} %get-tuple-element.19) | copy-start | bytes 6291460

commit v2 on v1

v2 whole, which is shorter than its diff:
```python
import functools

import jax
import jax.numpy as jnp
from jax import lax
from jax.experimental import pallas as pl
from jax.experimental.pallas import tpu as pltpu
from jax.sharding import Mesh
from jax.sharding import PartitionSpec as P

AXES = ("zl", "core", "zh", "xy")
EX = ("zl", "core")
EY = ("zh", "xy")
ALL = AXES
ZH = 2
LANES = 128
F32 = jnp.float32
BF16 = jnp.bfloat16


def dot(a, b, ca, cb):
    return lax.dot_general(a, b, (((ca,), (cb,)), ((), ())), preferred_element_type=F32)


def softmax_along(values, axis):
    top = jnp.max(values, axis=axis, keepdims=True)
    expo = jnp.exp(values - top)
    return expo / jnp.sum(expo, axis=axis, keepdims=True)


def gelu_parts(pre):
    cdf = 0.5 * (1.0 + lax.erf(pre * 0.7071067811865476))
    slope = cdf + pre * jnp.exp(-0.5 * pre * pre) * 0.3989422804014327
    return (pre * cdf, slope)


def kernel(
    ZL, XY,
    tok_hbm, par_hbm, wi_hbm, wo_hbm, go_hbm,
    gt_out, gp_out, gwi_out, gwo_out,
    tok, par, go, wi, wo,
    disp, comb, disp_b, comb_b,
    rows32, send1, recv1, planes, gathered,
    pre_s, slope_s, hid, dpre,
    ysend, yin, send2, recv2, slots,
    gwi_v, gwo_v,
    xsend, xrecv, zsend, zrecv, usend, urecv,
    in_sem, out_sem, w_send, w_recv, g_send, g_recv,
    a_send, a_recv, b_send, b_recv, y_send, y_recv, c_send, c_recv,
    x_send, x_recv, z_send, z_recv, u_send, u_recv,
):
    T = 2 * XY
    NZ = ZL * ZH
    S, D = par.shape
    J = D // LANES
    PAIR = 2 * J
    zl = lax.axis_index("zl")
    core = lax.axis_index("core")
    zh = lax.axis_index("zh")
    xy = lax.axis_index("xy")
    me_t = xy * 2 + core
    me_z = zh * ZL + zl

    def in_plane(d):
        t = lax.rem(me_t + d, T)
        return t, (zl, lax.rem(t, 2), zh, lax.div(t, 2))

    def along_z(d):
        z = lax.rem(me_z + d, NZ)
        return z, (lax.rem(z, ZL), core, lax.div(z, ZL), xy)

    sibling = (zl, 1 - core, zh, xy)

    def remote(src, dst, send_sem, recv_sem, device):
        return pltpu.make_async_remote_copy(
            src_ref=src, dst_ref=dst, send_sem=send_sem, recv_sem=recv_sem,
            device_id=device, device_id_type=pl.DeviceIdType.MESH,
        )

    barrier = pltpu.get_barrier_semaphore()

    def greet_plane(d, carry):
        pl.semaphore_signal(barrier, inc=1, device_id=in_plane(d)[1], device_id_type=pl.DeviceIdType.MESH)
        return carry

    def greet_z(d, carry):
        pl.semaphore_signal(barrier, inc=1, device_id=along_z(d)[1], device_id_type=pl.DeviceIdType.MESH)
        return carry

    loads = [
        pltpu.make_async_copy(tok_hbm, tok, in_sem.at[0]),
        pltpu.make_async_copy(par_hbm, par, in_sem.at[1]),
        pltpu.make_async_copy(go_hbm, go, in_sem.at[2]),
        pltpu.make_async_copy(wi_hbm.at[core], wi.at[core], in_sem.at[3]),
        pltpu.make_async_copy(wo_hbm.at[core], wo.at[core], in_sem.at[4]),
    ]
    for load in loads:
        load.start()
    lax.fori_loop(1, T, greet_plane, 0)
    lax.fori_loop(1, NZ, greet_z, 0)

    def pack(part, h, w):
        for j in range(J):
            rows32[pl.ds(h * PAIR + w * J + j, T, stride=ZH * PAIR), :] = part[:, j * LANES : (j + 1) * LANES]

    def unpack(h, w, j):
        return rows32[pl.ds(h * PAIR + w * J + j, T, stride=ZH * PAIR), :].astype(BF16)

    def all_to_all(send, recv, send_sem, recv_sem):
        def go_to(d, carry):
            t, device = in_plane(d)
            remote(send.at[t], recv.at[me_t], send_sem, recv_sem, device).start()
            return carry

        lax.fori_loop(1, T, go_to, 0)

    def wait_for(ref, sem):
        pltpu.make_async_copy(ref, ref, sem).wait()

    def wait_all(ref, count, sem):
        wait_for(ref.at[pl.ds(0, count)], sem)

    loads[0].wait()
    loads[1].wait()
    logits = dot(tok[...], par[...], 1, 1)
    dispatch = softmax_along(logits, 0)
    combine = softmax_along(logits, 1)
    disp[...] = dispatch
    comb[...] = combine
    disp_b[...] = dispatch.astype(BF16)
    comb_b[...] = combine.astype(BF16)
    slot_in = dot(disp_b[...], tok[...], 0, 0)
    for h in range(ZH):
        pack(slot_in[h * T : (h + 1) * T], h, 0)
    loads[2].wait()
    slot_cot = dot(comb_b[...], go[...], 0, 0)
    for h in range(ZH):
        pack(slot_cot[h * T : (h + 1) * T], h, 1)
    send1[...] = rows32[...].astype(BF16).reshape(send1.shape)

    pl.semaphore_wait(barrier, T - 1 + NZ - 1)
    all_to_all(send1, recv1, a_send, a_recv)
    swap = [
        remote(wi_hbm.at[1 - core], wi.at[core], w_send.at[0], w_recv.at[0], sibling),
        remote(wo_hbm.at[1 - core], wo.at[core], w_send.at[1], w_recv.at[1], sibling),
    ]
    for copy in swap:
        copy.start()
    wait_all(send1, T - 1, a_send)
    wait_all(recv1, T - 1, a_recv)
    recv1[me_t] = send1[me_t]
    rows32[...] = recv1[...].reshape(rows32.shape).astype(F32)
    for h in range(ZH):
        for w in range(2):
            for j in range(J):
                planes[h, w, :, j * LANES : (j + 1) * LANES] = unpack(h, w, j)
    for w in range(2):
        gathered[w, me_z] = planes[zh, w]

    def send_planes(w):
        def one(d, carry):
            z, device = along_z(d)
            remote(planes.at[lax.div(z, ZL), w], gathered.at[w, me_z], b_send.at[w], b_recv.at[w], device).start()
            return carry

        lax.fori_loop(1, NZ, one, 0)

    def send_back(w):
        def one(d, carry):
            z, device = along_z(d)
            remote(ysend.at[w, z], yin.at[w, me_z], y_send.at[w], y_recv.at[w], device).start()
            return carry

        lax.fori_loop(1, NZ, one, 0)
        yin[w, me_z] = ysend[w, me_z]

    send_planes(0)
    send_planes(1)
    for copy in loads[3:] + swap:
        copy.wait()

    rows = NZ * T
    step = min(16, rows)

    def by_rows(body):
        def one(k, carry):
            body(pl.ds(pl.multiple_of(k * step, step), step))
            return carry

        lax.fori_loop(0, rows // step, one, 0)

    def whole(w):
        return gathered[w].reshape(rows, D)

    def pre_part(f):
        pre_s[...] = dot(whole(0), wi[f], 1, 0)

        def body(part):
            value, slope = gelu_parts(pre_s[part, :])
            hid[f, part, :] = value.astype(BF16)
            slope_s[f, part, :] = slope

        by_rows(body)

    def back_part(f):
        pre_s[...] = dot(whole(1), wo[f], 1, 1)

        def body(part):
            dpre[f, part, :] = (pre_s[part, :] * slope_s[f, part, :]).astype(BF16)

        by_rows(body)

    def out_part(w):
        if w == 0:
            total = dot(hid[0], wo[0], 1, 0) + dot(hid[1], wo[1], 1, 0)
        else:
            total = dot(dpre[0], wi[0], 1, 1) + dot(dpre[1], wi[1], 1, 1)
        ysend[w] = total.astype(BF16).reshape(ysend.shape[1:])

    def win_part(f):
        gwi_v[f] = dot(whole(0), dpre[f], 0, 0).astype(BF16)

    def wout_part(f):
        gwo_v[f] = dot(hid[f], whole(1), 0, 0).astype(BF16)

    wait_all(gathered.at[0], NZ - 1, b_recv.at[0])
    pre_part(0)
    pre_part(1)
    out_part(0)
    send_back(0)
    wait_all(gathered.at[1], NZ - 1, b_recv.at[1])
    back_part(0)
    back_part(1)
    out_part(1)
    send_back(1)
    for f in range(2):
        wout_part(f)
        win_part(f)
    stores = [
        pltpu.make_async_copy(gwi_v.at[core], gwi_out.at[core], out_sem.at[0]),
        pltpu.make_async_copy(gwo_v.at[core], gwo_out.at[core], out_sem.at[1]),
        remote(gwi_v.at[1 - core], gwi_out.at[core], g_send.at[0], g_recv.at[0], sibling),
        remote(gwo_v.at[1 - core], gwo_out.at[core], g_send.at[1], g_recv.at[1], sibling),
    ]
    for copy in stores:
        copy.start()
    for w in range(2):
        wait_all(gathered.at[w], NZ - 1, b_send.at[w])
        wait_all(ysend.at[w], NZ - 1, y_send.at[w])

    for w in range(2):
        wait_all(yin.at[w], NZ - 1, y_recv.at[w])
        for h in range(ZH):
            pack(jnp.sum(yin[w, h * ZL : (h + 1) * ZL].astype(F32), axis=0), h, w)
    send2[...] = rows32[...].astype(BF16).reshape(send2.shape)
    all_to_all(send2, recv2, c_send, c_recv)
    wait_all(send2, T - 1, c_send)
    wait_all(recv2, T - 1, c_recv)
    recv2[me_t] = send2[me_t]
    rows32[...] = recv2[...].reshape(rows32.shape).astype(F32)
    for h in range(ZH):
        for w in range(2):
            for j in range(J):
                slots[w, h * T : (h + 1) * T, j * LANES : (j + 1) * LANES] = unpack(h, w, j)

    d_combine = dot(go[...], slots[0], 1, 1)
    d_dispatch = dot(tok[...], slots[1], 1, 1)
    dispatch = disp[...]
    combine = comb[...]
    d_logits = dispatch * (d_dispatch - jnp.sum(dispatch * d_dispatch, axis=0, keepdims=True))
    d_logits = d_logits + combine * (d_combine - jnp.sum(combine * d_combine, axis=1, keepdims=True))
    logit_grad = d_logits.astype(BF16)
    local_param = dot(logit_grad, tok[...], 0, 0)

    R = min(16, S)
    tiles = [
        (k * R // 16, slice(k * R % 16, k * R % 16 + R), slice(r, r + R), slice(j * LANES, (j + 1) * LANES))
        for k, (r, j) in enumerate((r, j) for r in range(0, S, R) for j in range(J))
    ]
    for k, inside, row, column in tiles:
        xsend[k, inside, :] = local_param[row, column].astype(BF16)
    all_to_all(xsend, xrecv, x_send, x_recv)
    gt_out[...] = (dot(disp_b[...], slots[1], 1, 0) + dot(logit_grad, par[...], 1, 0)).astype(BF16)
    wait_all(xsend, T - 1, x_send)
    wait_all(xrecv, T - 1, x_recv)
    xrecv[me_t] = xsend[me_t]
    zsend[...] = jnp.sum(xrecv[...].astype(F32), axis=0)

    def send_sum(d, carry):
        remote(zsend, zrecv.at[me_z], z_send, z_recv, along_z(d)[1]).start()
        return carry

    lax.fori_loop(1, NZ, send_sum, 0)
    wait_all(zrecv, NZ - 1, z_send)
    wait_all(zrecv, NZ - 1, z_recv)
    zrecv[me_z] = zsend[...]
    usend[...] = jnp.sum(zrecv[...], axis=0).astype(BF16)

    def send_total(d, carry):
        remote(usend, urecv.at[me_t], u_send, u_recv, in_plane(d)[1]).start()
        return carry

    lax.fori_loop(1, T, send_total, 0)
    wait_all(urecv, T - 1, u_send)
    wait_all(urecv, T - 1, u_recv)
    urecv[me_t] = usend[...]
    for k, inside, row, column in tiles:
        gp_out[row, column] = urecv[k, inside, :].astype(F32)
    for copy in stores:
        copy.wait()


def deliver(gt, gp, gwi, gwo, gt_out, gp_out, gwi_out, gwo_out, gt_v, gp_v, gwi_v, gwo_v, in_sem, out_sem):
    parts = []
    for src, held, dst in ((gwi, gwi_v, gwi_out), (gwo, gwo_v, gwo_out)):
        half = src.shape[1] // 2
        for e in range(2):
            for low in (0, half):
                at = (e, pl.ds(low, half))
                parts.append((src.at[at], held.at[at], dst.at[at]))
    parts += [(gt, gt_v, gt_out), (gp, gp_v, gp_out)]
    ins = [pltpu.make_async_copy(src, held, in_sem.at[k]) for k, (src, held, _) in enumerate(parts)]
    outs = [pltpu.make_async_copy(held, dst, out_sem.at[k]) for k, (_, held, dst) in enumerate(parts)]
    for copy in ins:
        copy.start()
    for came, goes in zip(ins, outs):
        came.wait()
        goes.start()
    for copy in outs:
        copy.wait()


def per_device(ZL, XY, tokens, slot_param, weight_in, weight_out, grad_out):
    _, patches, D = tokens.shape
    S = slot_param.shape[1]
    F = weight_in.shape[2]
    T = 2 * XY
    NZ = ZL * ZH
    rows = NZ * T
    PAIR = 2 * (D // LANES)
    DMA = pltpu.SemaphoreType.DMA
    vmem = pltpu.VMEM
    anywhere = pl.BlockSpec(memory_space=pl.ANY)
    in_hbm = pl.BlockSpec(memory_space=pltpu.HBM)
    in_vmem = pl.BlockSpec(memory_space=pltpu.VMEM)
    scratch = [
        vmem((patches, D), BF16), vmem((S, D), BF16), vmem((patches, D), BF16),
        vmem((2, D, F), BF16), vmem((2, F, D), BF16),
        vmem((patches, S), F32), vmem((patches, S), F32), vmem((patches, S), BF16), vmem((patches, S), BF16),
        vmem((T * ZH * PAIR, LANES), F32),
        vmem((T, ZH * PAIR, LANES), BF16), vmem((T, ZH * PAIR, LANES), BF16),
        vmem((ZH, 2, T, D), BF16), vmem((2, NZ, T, D), BF16),
        vmem((rows, F), F32), vmem((2, rows, F), F32), vmem((2, rows, F), BF16), vmem((2, rows, F), BF16),
        vmem((2, NZ, T, D), BF16), vmem((2, NZ, T, D), BF16),
        vmem((T, ZH * PAIR, LANES), BF16), vmem((T, ZH * PAIR, LANES), BF16),
        vmem((2, S, D), BF16),
        vmem((2, D, F), BF16), vmem((2, F, D), BF16),
        vmem((T, 16, LANES), BF16), vmem((T, 16, LANES), BF16),
        vmem((16, LANES), F32), vmem((NZ, 16, LANES), F32),
        vmem((16, LANES), BF16), vmem((T, 16, LANES), BF16),
        DMA((5,)), DMA((2,)), DMA((2,)), DMA((2,)), DMA((2,)), DMA((2,)),
        DMA, DMA, DMA((2,)), DMA((2,)), DMA((2,)), DMA((2,)), DMA, DMA,
        DMA, DMA, DMA, DMA, DMA, DMA,
    ]
    shapes = (
        jax.ShapeDtypeStruct((patches, D), BF16),
        jax.ShapeDtypeStruct((S, D), F32),
        jax.ShapeDtypeStruct(weight_in.shape, BF16),
        jax.ShapeDtypeStruct(weight_out.shape, BF16),
    )
    results = pl.pallas_call(
        functools.partial(kernel, ZL, XY),
        out_shape=shapes,
        in_specs=[in_hbm] * 5,
        out_specs=[in_vmem, in_vmem, anywhere, anywhere],
        scratch_shapes=scratch,
        compiler_params=pltpu.CompilerParams(
            collective_id=0, has_side_effects=True, vmem_limit_bytes=60 * 1024 * 1024
        ),
    )(tokens[0], slot_param.T, weight_in, weight_out, grad_out[0])
    grad_tokens, grad_param, grad_win, grad_wout = pl.pallas_call(
        deliver,
        out_shape=shapes,
        in_specs=[anywhere] * 4,
        out_specs=[in_hbm] * 4,
        scratch_shapes=[vmem(shape.shape, shape.dtype) for shape in shapes] + [DMA((10,)), DMA((10,))],
        compiler_params=pltpu.CompilerParams(vmem_limit_bytes=60 * 1024 * 1024),
    )(*results)
    return grad_tokens[None], grad_param.T, grad_win, grad_wout


def solution(mesh):
    ZL = mesh.shape["ex"] // 2
    XY = mesh.shape["ey"] // ZH
    split = Mesh(mesh.devices.reshape(ZL, 2, ZH, XY), AXES)
    return jax.shard_map(
        functools.partial(per_device, ZL, XY),
        mesh=split,
        in_specs=(P(ALL, None, None), P(), P(EY, None, EX), P(EY, EX, None), P(ALL, None, None)),
        out_specs=(P(ALL, None, None), P(), P(EY, None, EX), P(EY, EX, None)),
        check_vma=False,
    )
```

time: 106 us -> 93.9 us (0.89)
  local copies, waits for them, and re-layouts: 8.32 us -> 0 us
  Pallas kernels: 96.6 us -> 93.2 us
    unnamed x11 -> x0, local copies, waits for them, and re-layouts: 8.32 us -> none
    pallas_call x1 -> x2, Pallas kernels: 96.6 us -> 93.2 us  [the longest x1 88.9 us: per_device(): pl.pallas_call(functools.partial(kernel, ZL, XY), out_shape=shapes, in_sp...]
where the time goes in v2:
time: 93.9 us; the launch traced here: 93.8 us
  Pallas kernels  93.2 us (99%)
    pallas_call x1, Pallas kernels, per_device(): pl.pallas_call(functools.partial(kernel, ZL, XY), out_shape=shapes, in_sp...  88.9 us
    pallas_call x1, Pallas kernels, per_device(): pl.pallas_call(deliver, out_shape=shapes, in_specs=[anywhere] * 4, out_sp...  4.34 us

profile of v2, /device:TPU:1, one launch (start us, length us, event | category | flops | bytes accessed | tf_op | source)
XLA Modules:
  0.0 93.8 jit_solution(5614540828941491348)
XLA Ops:
  0.6 88.9 %shard_map.84 = (bf16[256,1024]{1,0:T(8,128)(2,1)}, f32[64,1024]{1,0:T(8,128)}, bf16[2,1024,512]{2,1,0:T(8,128)(2,1)}, bf16[2,512,1024]{2,1,0:T(8,128)(2,1)}) custom-call(bf16[256,1024]{1,0:T(8,128)(2,1)} %bitcast.5, bf16[64,1024]{1,0:T(8,128)(2,1)} %bitcast.7, bf16[2,1024,512]{2,1,0:T(8,128)(2,1)} %wi_hbm.1, bf16[2,512,1024]{2,1,0:T(8,128)(2,1)} %wo_hbm.1, ...), custom_call_target="tpu_custom_call" | custom-call | tf_op jit(solution)/shard_map/pallas_call | solution.py:371
  89.5 4.3 %shard_map.85 = (bf16[256,1024]{1,0:T(8,128)(2,1)}, f32[64,1024]{1,0:T(8,128)}, bf16[2,1024,512]{2,1,0:T(8,128)(2,1)}, bf16[2,512,1024]{2,1,0:T(8,128)(2,1)}) custom-call(bf16[256,1024]{1,0:T(8,128)(2,1)} %get-tuple-element.12.gt, f32[64,1024]{1,0:T(8,128)} %get-tuple-element.13.gp, bf16[2,1024,512]{2,1,0:T(8,128)(2,1)} %get-tuple-element.14.gwi, ...), custom_call_target="tpu_custom_call" | custom-call | tf_op jit(solution)/shard_map/pallas_call | solution.py:381

commit v3 on v2

--- a/solution.py
+++ b/solution.py
@@ -42,7 +42,7 @@
     disp, comb, disp_b, comb_b,
     rows32, send1, recv1, planes, gathered,
     pre_s, slope_s, hid, dpre,
-    ysend, yin, send2, recv2, slots,
+    ysend, yin, ypair, fin, send2, recv2, slots,
     gwi_v, gwo_v,
     xsend, xrecv, zsend, zrecv, usend, urecv,
     in_sem, out_sem, w_send, w_recv, g_send, g_recv,
@@ -53,7 +53,6 @@
     NZ = ZL * ZH
     S, D = par.shape
     J = D // LANES
-    PAIR = 2 * J
     zl = lax.axis_index("zl")
     core = lax.axis_index("core")
     zh = lax.axis_index("zh")
@@ -101,10 +100,17 @@
 
     def pack(part, h, w):
         for j in range(J):
-            rows32[pl.ds(h * PAIR + w * J + j, T, stride=ZH * PAIR), :] = part[:, j * LANES : (j + 1) * LANES]
+            rows32[w, pl.ds(h * J + j, T, stride=ZH * J), :] = part[:, j * LANES : (j + 1) * LANES]
+
+    def messages(w):
+        return rows32[w].reshape(T, ZH * J, LANES).astype(BF16)
 
     def unpack(h, w, j):
-        return rows32[pl.ds(h * PAIR + w * J + j, T, stride=ZH * PAIR), :].astype(BF16)
+        return rows32[w, pl.ds(h * J + j, T, stride=ZH * J), :].astype(BF16)
+
+    def arrived(send, recv, w):
+        recv[w, me_t] = send[w, me_t]
+        rows32[w] = recv[w].reshape(T * ZH * J, LANES).astype(F32)
 
     def all_to_all(send, recv, send_sem, recv_sem):
         def go_to(d, carry):
@@ -124,60 +130,99 @@
     loads[1].wait()
     logits = dot(tok[...], par[...], 1, 1)
     dispatch = softmax_along(logits, 0)
-    combine = softmax_along(logits, 1)
     disp[...] = dispatch
-    comb[...] = combine
     disp_b[...] = dispatch.astype(BF16)
-    comb_b[...] = combine.astype(BF16)
     slot_in = dot(disp_b[...], tok[...], 0, 0)
     for h in range(ZH):
         pack(slot_in[h * T : (h + 1) * T], h, 0)
+    send1[0] = messages(0)
+    pl.semaphore_wait(barrier, T - 1 + NZ - 1)
+    all_to_all(send1.at[0], recv1.at[0], a_send.at[0], a_recv.at[0])
+    combine = softmax_along(logits, 1)
+    comb[...] = combine
+    comb_b[...] = combine.astype(BF16)
     loads[2].wait()
     slot_cot = dot(comb_b[...], go[...], 0, 0)
     for h in range(ZH):
         pack(slot_cot[h * T : (h + 1) * T], h, 1)
-    send1[...] = rows32[...].astype(BF16).reshape(send1.shape)
-
-    pl.semaphore_wait(barrier, T - 1 + NZ - 1)
-    all_to_all(send1, recv1, a_send, a_recv)
+    send1[1] = messages(1)
+    all_to_all(send1.at[1], recv1.at[1], a_send.at[1], a_recv.at[1])
     swap = [
         remote(wi_hbm.at[1 - core], wi.at[core], w_send.at[0], w_recv.at[0], sibling),
         remote(wo_hbm.at[1 - core], wo.at[core], w_send.at[1], w_recv.at[1], sibling),
     ]
     for copy in swap:
         copy.start()
-    wait_all(send1, T - 1, a_send)
-    wait_all(recv1, T - 1, a_recv)
-    recv1[me_t] = send1[me_t]
-    rows32[...] = recv1[...].reshape(rows32.shape).astype(F32)
-    for h in range(ZH):
-        for w in range(2):
+
+    odd = lax.rem(zl, 2)
+    partner = (zl + 1 - 2 * odd, core, zh, xy)
+    mine = (1 - zh) * ZL + 2 * (1 - odd)
+    theirs = (1 - zh) * ZL + 2 * odd
+
+    def in_group(d):
+        k = lax.rem(zl + d, ZL)
+        return zh * ZL + k, (k, core, zh, xy)
+
+    def send_planes(w):
+        wait_all(send1.at[w], T - 1, a_send.at[w])
+        wait_all(recv1.at[w], T - 1, a_recv.at[w])
+        arrived(send1, recv1, w)
+        for h in range(ZH):
             for j in range(J):
                 planes[h, w, :, j * LANES : (j + 1) * LANES] = unpack(h, w, j)
-    for w in range(2):
+        first = 1 - lax.div(zl, 2)
+        for k in range(2):
+            device = (first + 2 * k, core, 1 - zh, xy)
+            remote(planes.at[1 - zh, w], gathered.at[w, me_z], b_send.at[w, 0], b_recv.at[w, 1], device).start()
+        for d in (2, 1, 3):
+            remote(planes.at[zh, w], gathered.at[w, me_z], b_send.at[w, 0], b_recv.at[w, 0], in_group(d)[1]).start()
         gathered[w, me_z] = planes[zh, w]
 
-    def send_planes(w):
-        def one(d, carry):
-            z, device = along_z(d)
-            remote(planes.at[lax.div(z, ZL), w], gathered.at[w, me_z], b_send.at[w], b_recv.at[w], device).start()
-            return carry
-
-        lax.fori_loop(1, NZ, one, 0)
+    def pass_on(w):
+        block = gathered.at[w, pl.ds(mine, 2)]
+        wait_for(block, b_recv.at[w, 1])
+        remote(block, block, b_send.at[w, 1], b_recv.at[w, 2], partner).start()
+
+    def all_here(w):
+        wait_for(gathered.at[w, pl.ds(zh * ZL, ZL - 1)], b_recv.at[w, 0])
+        wait_for(gathered.at[w, pl.ds(theirs, 2)], b_recv.at[w, 2])
 
     def send_back(w):
-        def one(d, carry):
-            z, device = along_z(d)
-            remote(ysend.at[w, z], yin.at[w, me_z], y_send.at[w], y_recv.at[w], device).start()
-            return carry
-
-        lax.fori_loop(1, NZ, one, 0)
-        yin[w, me_z] = ysend[w, me_z]
+        remote(ysend.at[w, pl.ds(theirs, 2)], ypair.at[w], y_send.at[w, 1], y_recv.at[w, 1], partner).start()
+        for d in (2, 1, 3):
+            z, device = in_group(d)
+            remote(ysend.at[w, z], yin.at[w, zl], y_send.at[w, 0], y_recv.at[w, 0], device).start()
+        yin[w, zl] = ysend[w, me_z]
+
+    def send_pairs(w):
+        wait_for(ypair.at[w], y_recv.at[w, 1])
+        for k in range(2):
+            ysend[w, mine + k] = (ysend[w, mine + k].astype(F32) + ypair[w, k].astype(F32)).astype(BF16)
+            device = (2 * (1 - odd) + k, core, 1 - zh, xy)
+            remote(ysend.at[w, mine + k], yin.at[w, ZL + lax.div(zl, 2)], y_send.at[w, 2], y_recv.at[w, 2], device).start()
+
+    def sums_back(w):
+        wait_for(yin.at[w, pl.ds(0, ZL - 1)], y_recv.at[w, 0])
+        wait_for(yin.at[w, pl.ds(ZL, 2)], y_recv.at[w, 2])
+        fin[zh] = jnp.sum(yin[w, :ZL].astype(F32), axis=0)
+        fin[1 - zh] = yin[w, ZL].astype(F32) + yin[w, ZL + 1].astype(F32)
+        for h in range(ZH):
+            pack(fin[h], h, w)
+        send2[w] = messages(w)
+        all_to_all(send2.at[w], recv2.at[w], c_send.at[w], c_recv.at[w])
+
+    def take_slots(w):
+        wait_all(recv2.at[w], T - 1, c_recv.at[w])
+        arrived(send2, recv2, w)
+        for h in range(ZH):
+            for j in range(J):
+                slots[w, h * T : (h + 1) * T, j * LANES : (j + 1) * LANES] = unpack(h, w, j)
 
     send_planes(0)
     send_planes(1)
     for copy in loads[3:] + swap:
         copy.wait()
+    pass_on(0)
 
     rows = NZ * T
     step = min(16, rows)
@@ -223,18 +268,22 @@
     def wout_part(f):
         gwo_v[f] = dot(hid[f], whole(1), 0, 0).astype(BF16)
 
-    wait_all(gathered.at[0], NZ - 1, b_recv.at[0])
+    all_here(0)
     pre_part(0)
+    pass_on(1)
     pre_part(1)
     out_part(0)
     send_back(0)
-    wait_all(gathered.at[1], NZ - 1, b_recv.at[1])
+    all_here(1)
     back_part(0)
+    send_pairs(0)
     back_part(1)
     out_part(1)
     send_back(1)
     for f in range(2):
         wout_part(f)
+    send_pairs(1)
+    for f in range(2):
         win_part(f)
     stores = [
         pltpu.make_async_copy(gwi_v.at[core], gwi_out.at[core], out_sem.at[0]),
@@ -244,31 +293,25 @@
     ]
     for copy in stores:
         copy.start()
+
+    sums_back(0)
+    take_slots(0)
+    d_combine = dot(go[...], slots[0], 1, 1)
+    combine = comb[...]
+    by_combine = combine * (d_combine - jnp.sum(combine * d_combine, axis=1, keepdims=True))
+    sums_back(1)
     for w in range(2):
-        wait_all(gathered.at[w], NZ - 1, b_send.at[w])
-        wait_all(ysend.at[w], NZ - 1, y_send.at[w])
-
-    for w in range(2):
-        wait_all(yin.at[w], NZ - 1, y_recv.at[w])
-        for h in range(ZH):
-            pack(jnp.sum(yin[w, h * ZL : (h + 1) * ZL].astype(F32), axis=0), h, w)
-    send2[...] = rows32[...].astype(BF16).reshape(send2.shape)
-    all_to_all(send2, recv2, c_send, c_recv)
-    wait_all(send2, T - 1, c_send)
-    wait_all(recv2, T - 1, c_recv)
-    recv2[me_t] = send2[me_t]
-    rows32[...] = recv2[...].reshape(rows32.shape).astype(F32)
-    for h in range(ZH):
-        for w in range(2):
-            for j in range(J):
-                slots[w, h * T : (h + 1) * T, j * LANES : (j + 1) * LANES] = unpack(h, w, j)
-
-    d_combine = dot(go[...], slots[0], 1, 1)
+        wait_all(gathered.at[w], ZL - 1 + 2, b_send.at[w, 0])
+        wait_all(gathered.at[w], 2, b_send.at[w, 1])
+        wait_all(ysend.at[w], ZL - 1, y_send.at[w, 0])
+        wait_all(ysend.at[w], 2, y_send.at[w, 1])
+        wait_all(ysend.at[w], 2, y_send.at[w, 2])
+        wait_all(send2.at[w], T - 1, c_send.at[w])
+    take_slots(1)
     d_dispatch = dot(tok[...], slots[1], 1, 1)
     dispatch = disp[...]
-    combine = comb[...]
     d_logits = dispatch * (d_dispatch - jnp.sum(dispatch * d_dispatch, axis=0, keepdims=True))
-    d_logits = d_logits + combine * (d_combine - jnp.sum(combine * d_combine, axis=1, keepdims=True))
+    d_logits = d_logits + by_combine
     logit_grad = d_logits.astype(BF16)
     local_param = dot(logit_grad, tok[...], 0, 0)
 
@@ -284,7 +327,7 @@
     wait_all(xsend, T - 1, x_send)
     wait_all(xrecv, T - 1, x_recv)
     xrecv[me_t] = xsend[me_t]
-    zsend[...] = jnp.sum(xrecv[...].astype(F32), axis=0)
+    zsend[...] = jnp.sum(xrecv[...].astype(F32), axis=0).astype(BF16)
 
     def send_sum(d, carry):
         remote(zsend, zrecv.at[me_z], z_send, z_recv, along_z(d)[1]).start()
@@ -294,7 +337,7 @@
     wait_all(zrecv, NZ - 1, z_send)
     wait_all(zrecv, NZ - 1, z_recv)
     zrecv[me_z] = zsend[...]
-    usend[...] = jnp.sum(zrecv[...], axis=0).astype(BF16)
+    usend[...] = jnp.sum(zrecv[...].astype(F32), axis=0).astype(BF16)
 
     def send_total(d, carry):
         remote(usend, urecv.at[me_t], u_send, u_recv, in_plane(d)[1]).start()
@@ -337,7 +380,7 @@
     T = 2 * XY
     NZ = ZL * ZH
     rows = NZ * T
-    PAIR = 2 * (D // LANES)
+    PER = ZH * (D // LANES)
     DMA = pltpu.SemaphoreType.DMA
     vmem = pltpu.VMEM
     anywhere = pl.BlockSpec(memory_space=pl.ANY)
@@ -347,19 +390,18 @@
         vmem((patches, D), BF16), vmem((S, D), BF16), vmem((patches, D), BF16),
         vmem((2, D, F), BF16), vmem((2, F, D), BF16),
         vmem((patches, S), F32), vmem((patches, S), F32), vmem((patches, S), BF16), vmem((patches, S), BF16),
-        vmem((T * ZH * PAIR, LANES), F32),
-        vmem((T, ZH * PAIR, LANES), BF16), vmem((T, ZH * PAIR, LANES), BF16),
+        vmem((2, T * PER, LANES), F32), vmem((2, T, PER, LANES), BF16), vmem((2, T, PER, LANES), BF16),
         vmem((ZH, 2, T, D), BF16), vmem((2, NZ, T, D), BF16),
         vmem((rows, F), F32), vmem((2, rows, F), F32), vmem((2, rows, F), BF16), vmem((2, rows, F), BF16),
-        vmem((2, NZ, T, D), BF16), vmem((2, NZ, T, D), BF16),
-        vmem((T, ZH * PAIR, LANES), BF16), vmem((T, ZH * PAIR, LANES), BF16),
+        vmem((2, NZ, T, D), BF16), vmem((2, ZL + 2, T, D), BF16), vmem((2, 2, T, D), BF16), vmem((ZH, T, D), F32),
+        vmem((2, T, PER, LANES), BF16), vmem((2, T, PER, LANES), BF16),
         vmem((2, S, D), BF16),
         vmem((2, D, F), BF16), vmem((2, F, D), BF16),
         vmem((T, 16, LANES), BF16), vmem((T, 16, LANES), BF16),
-        vmem((16, LANES), F32), vmem((NZ, 16, LANES), F32),
+        vmem((16, LANES), BF16), vmem((NZ, 16, LANES), BF16),
         vmem((16, LANES), BF16), vmem((T, 16, LANES), BF16),
         DMA((5,)), DMA((2,)), DMA((2,)), DMA((2,)), DMA((2,)), DMA((2,)),
-        DMA, DMA, DMA((2,)), DMA((2,)), DMA((2,)), DMA((2,)), DMA, DMA,
+        DMA((2,)), DMA((2,)), DMA((2, 2)), DMA((2, 3)), DMA((2, 3)), DMA((2, 3)), DMA((2,)), DMA((2,)),
         DMA, DMA, DMA, DMA, DMA, DMA,
     ]
     shapes = (

time: 93.9 us -> 91.5 us (0.974)
  Pallas kernels: 93.2 us -> 90.7 us
    pallas_call x1, Pallas kernels: 88.9 us -> 86.4 us  [per_device(): pl.pallas_call(functools.partial(kernel, ZL, XY), out_shape=shapes, in_sp...]
where the time goes in v3:
time: 91.5 us; the launch traced here: 91.4 us
  Pallas kernels  90.7 us (99%)
    pallas_call x1, Pallas kernels, per_device(): pl.pallas_call(functools.partial(kernel, ZL, XY), out_shape=shapes, in_sp...  86.4 us
    pallas_call x1, Pallas kernels, per_device(): pl.pallas_call(deliver, out_shape=shapes, in_specs=[anywhere] * 4, out_sp...  4.34 us

profile of v3, /device:TPU:1, one launch (start us, length us, event | category | flops | bytes accessed | tf_op | source)
XLA Modules:
  0.0 91.4 jit_solution(7208639291967039168)
XLA Ops:
  0.6 86.4 %shard_map.84 = (bf16[256,1024]{1,0:T(8,128)(2,1)}, f32[64,1024]{1,0:T(8,128)}, bf16[2,1024,512]{2,1,0:T(8,128)(2,1)}, bf16[2,512,1024]{2,1,0:T(8,128)(2,1)}) custom-call(bf16[256,1024]{1,0:T(8,128)(2,1)} %bitcast.5, bf16[64,1024]{1,0:T(8,128)(2,1)} %bitcast.7, bf16[2,1024,512]{2,1,0:T(8,128)(2,1)} %wi_hbm.1, bf16[2,512,1024]{2,1,0:T(8,128)(2,1)} %wo_hbm.1, ...), custom_call_target="tpu_custom_call" | custom-call | tf_op jit(solution)/shard_map/pallas_call | solution.py:413
  87.0 4.3 %shard_map.85 = (bf16[256,1024]{1,0:T(8,128)(2,1)}, f32[64,1024]{1,0:T(8,128)}, bf16[2,1024,512]{2,1,0:T(8,128)(2,1)}, bf16[2,512,1024]{2,1,0:T(8,128)(2,1)}) custom-call(bf16[256,1024]{1,0:T(8,128)(2,1)} %get-tuple-element.12.gt, f32[64,1024]{1,0:T(8,128)} %get-tuple-element.13.gp, bf16[2,1024,512]{2,1,0:T(8,128)(2,1)} %get-tuple-element.14.gwi, ...), custom_call_target="tpu_custom_call" | custom-call | tf_op jit(solution)/shard_map/pallas_call | solution.py:423

commit v4 on v3

--- a/solution.py
+++ b/solution.py
@@ -353,23 +353,12 @@
         copy.wait()
 
 
-def deliver(gt, gp, gwi, gwo, gt_out, gp_out, gwi_out, gwo_out, gt_v, gp_v, gwi_v, gwo_v, in_sem, out_sem):
-    parts = []
-    for src, held, dst in ((gwi, gwi_v, gwi_out), (gwo, gwo_v, gwo_out)):
-        half = src.shape[1] // 2
-        for e in range(2):
-            for low in (0, half):
-                at = (e, pl.ds(low, half))
-                parts.append((src.at[at], held.at[at], dst.at[at]))
-    parts += [(gt, gt_v, gt_out), (gp, gp_v, gp_out)]
-    ins = [pltpu.make_async_copy(src, held, in_sem.at[k]) for k, (src, held, _) in enumerate(parts)]
-    outs = [pltpu.make_async_copy(held, dst, out_sem.at[k]) for k, (_, held, dst) in enumerate(parts)]
-    for copy in ins:
+def deliver(gt, gp, gwi, gwo, gt_out, gp_out, gwi_out, gwo_out, sem):
+    pairs = ((gwi, gwi_out), (gwo, gwo_out), (gt, gt_out), (gp, gp_out))
+    copies = [pltpu.make_async_copy(src, dst, sem.at[k]) for k, (src, dst) in enumerate(pairs)]
+    for copy in copies:
         copy.start()
-    for came, goes in zip(ins, outs):
-        came.wait()
-        goes.start()
-    for copy in outs:
+    for copy in copies:
         copy.wait()
 
 
@@ -417,16 +406,16 @@
         out_specs=[in_vmem, in_vmem, anywhere, anywhere],
         scratch_shapes=scratch,
         compiler_params=pltpu.CompilerParams(
-            collective_id=0, has_side_effects=True, vmem_limit_bytes=60 * 1024 * 1024
+            collective_id=0, has_side_effects=True, vmem_limit_bytes=40 * 1024 * 1024
         ),
-    )(tokens[0], slot_param.T, weight_in, weight_out, grad_out[0])
+    )(*(pltpu.with_memory_space_constraint(x, pltpu.HBM) for x in (tokens[0], slot_param.T, weight_in, weight_out, grad_out[0])))
     grad_tokens, grad_param, grad_win, grad_wout = pl.pallas_call(
         deliver,
         out_shape=shapes,
         in_specs=[anywhere] * 4,
         out_specs=[in_hbm] * 4,
-        scratch_shapes=[vmem(shape.shape, shape.dtype) for shape in shapes] + [DMA((10,)), DMA((10,))],
-        compiler_params=pltpu.CompilerParams(vmem_limit_bytes=60 * 1024 * 1024),
+        scratch_shapes=[DMA((4,))],
+        compiler_params=pltpu.CompilerParams(vmem_limit_bytes=1024 * 1024),
     )(*results)
     return grad_tokens[None], grad_param.T, grad_win, grad_wout
 

time: 91.5 us -> 88.8 us (0.970)
  Pallas kernels: 90.7 us -> 88 us
    pallas_call x1, Pallas kernels: 4.34 us -> 2.28 us  [per_device(): pl.pallas_call(deliver, out_shape=shapes, in_specs=[anywhere] * 4, out_sp...]
where the time goes in v4:
time: 88.8 us; the launch traced here: 88.7 us
  Pallas kernels  88 us (99%)
    pallas_call x1, Pallas kernels, per_device(): pl.pallas_call(functools.partial(kernel, ZL, XY), out_shape=shapes, in_sp...  85.8 us
    pallas_call x1, Pallas kernels, per_device(): pl.pallas_call(deliver, out_shape=shapes, in_specs=[anywhere] * 4, out_sp...  2.28 us

profile of v4, /device:TPU:1, one launch (start us, length us, event | category | flops | bytes accessed | tf_op | source)
XLA Modules:
  0.0 88.7 jit_solution(11318356083288780375)
XLA Ops:
  0.6 85.8 %shard_map.84 = (bf16[256,1024]{1,0:T(8,128)(2,1)S(1)}, f32[64,1024]{1,0:T(8,128)S(1)}, bf16[2,1024,512]{2,1,0:T(8,128)(2,1)S(1)}, bf16[2,512,1024]{2,1,0:T(8,128)(2,1)S(1)}) custom-call(bf16[256,1024]{1,0:T(8,128)(2,1)} %bitcast.5, bf16[64,1024]{1,0:T(8,128)(2,1)} %bitcast.7, bf16[2,1024,512]{2,1,0:T(8,128)(2,1)} %wi_hbm.1, bf16[2,512,1024]{2,1,0:T(8,128)(2,1)} %wo_hbm.1, ...), custom_call_target="tpu_custom_call" | custom-call | tf_op jit(solution)/shard_map/pallas_call | solution.py:402
  86.4 2.3 %shard_map.85 = (bf16[256,1024]{1,0:T(8,128)(2,1)}, f32[64,1024]{1,0:T(8,128)}, bf16[2,1024,512]{2,1,0:T(8,128)(2,1)}, bf16[2,512,1024]{2,1,0:T(8,128)(2,1)}) custom-call(bf16[256,1024]{1,0:T(8,128)(2,1)S(1)} %get-tuple-element.12.gt, f32[64,1024]{1,0:T(8,128)S(1)} %get-tuple-element.13.gp, bf16[2,1024,512]{2,1,0:T(8,128)(2,1)S(1)} %get-tuple-element.14.gwi, ...), custom_call_target="tpu_custom_call" | custom-call | tf_op jit(solution)/shard_map/pallas_call | solution.py:412

commit v5 on v4

--- a/solution.py
+++ b/solution.py
@@ -61,7 +61,7 @@
     me_z = zh * ZL + zl
 
     def in_plane(d):
-        t = lax.rem(me_t + d, T)
+        t = lax.rem(me_t + 11 * d, T)
         return t, (zl, lax.rem(t, 2), zh, lax.div(t, 2))
 
     def along_z(d):
@@ -170,22 +170,66 @@
         for h in range(ZH):
             for j in range(J):
                 planes[h, w, :, j * LANES : (j + 1) * LANES] = unpack(h, w, j)
-        first = 1 - lax.div(zl, 2)
-        for k in range(2):
-            device = (first + 2 * k, core, 1 - zh, xy)
-            remote(planes.at[1 - zh, w], gathered.at[w, me_z], b_send.at[w, 0], b_recv.at[w, 1], device).start()
+        device = (3 * (1 - lax.div(zl, 2)), core, 1 - zh, xy)
+        remote(planes.at[1 - zh, w], gathered.at[w, me_z], b_send.at[w], b_recv.at[w, ZL + lax.div(zl, 2)], device).start()
         for d in (2, 1, 3):
-            remote(planes.at[zh, w], gathered.at[w, me_z], b_send.at[w, 0], b_recv.at[w, 0], in_group(d)[1]).start()
+
+            @pl.when(zl != {1: ZL - 1, 2: ZL, 3: 0}[d])
+            def _(d=d):
+                remote(planes.at[zh, w], gathered.at[w, me_z], b_send.at[w], b_recv.at[w, zl], in_group(d)[1]).start()
+
         gathered[w, me_z] = planes[zh, w]
 
+    def own(w, k):
+        return gathered.at[w, zh * ZL + k]
+
+    def pair(w, k):
+        return gathered.at[w, pl.ds((1 - zh) * ZL + 2 * k, 2)]
+
+    def to_place(block, w, sem, k):
+        remote(block, block, b_send.at[w], b_recv.at[w, sem], (k, core, zh, xy)).start()
+
+    def take_own(w, k):
+        wait_for(own(w, k), b_recv.at[w, k])
+
+    def take_pair(w, k):
+        wait_for(pair(w, k), b_recv.at[w, ZL + k])
+
     def pass_on(w):
-        block = gathered.at[w, pl.ds(mine, 2)]
-        wait_for(block, b_recv.at[w, 1])
-        remote(block, block, b_send.at[w, 1], b_recv.at[w, 2], partner).start()
+        @pl.when(zl == 0)
+        def _():
+            take_pair(w, 1)
+            to_place(pair(w, 1), w, ZL + 1, 2)
+            to_place(pair(w, 1), w, ZL + 1, 1)
+
+        @pl.when(zl == 3)
+        def _():
+            take_pair(w, 0)
+            to_place(pair(w, 0), w, ZL, 1)
+            to_place(pair(w, 0), w, ZL, 2)
+
+        @pl.when(zl == 1)
+        def _():
+            take_own(w, 3)
+            to_place(own(w, 3), w, 3, 0)
+            take_pair(w, 0)
+            to_place(pair(w, 0), w, ZL, 0)
+
+        @pl.when(zl == 2)
+        def _():
+            take_own(w, 0)
+            to_place(own(w, 0), w, 0, 3)
+            take_pair(w, 1)
+            to_place(pair(w, 1), w, ZL + 1, 3)
 
     def all_here(w):
-        wait_for(gathered.at[w, pl.ds(zh * ZL, ZL - 1)], b_recv.at[w, 0])
-        wait_for(gathered.at[w, pl.ds(theirs, 2)], b_recv.at[w, 2])
+        for p, left, last in ((0, (1, 2, 3), 0), (1, (0, 2), 1), (2, (1, 3), 0), (3, (0, 1, 2), 1)):
+
+            @pl.when(zl == p)
+            def _(left=left, last=last):
+                for k in left:
+                    take_own(w, k)
+                take_pair(w, last)
 
     def send_back(w):
         remote(ysend.at[w, pl.ds(theirs, 2)], ypair.at[w], y_send.at[w, 1], y_recv.at[w, 1], partner).start()
@@ -268,9 +312,9 @@
     def wout_part(f):
         gwo_v[f] = dot(hid[f], whole(1), 0, 0).astype(BF16)
 
+    pass_on(1)
     all_here(0)
     pre_part(0)
-    pass_on(1)
     pre_part(1)
     out_part(0)
     send_back(0)
@@ -301,8 +345,7 @@
     by_combine = combine * (d_combine - jnp.sum(combine * d_combine, axis=1, keepdims=True))
     sums_back(1)
     for w in range(2):
-        wait_all(gathered.at[w], ZL - 1 + 2, b_send.at[w, 0])
-        wait_all(gathered.at[w], 2, b_send.at[w, 1])
+        wait_all(gathered.at[w], 7, b_send.at[w])
         wait_all(ysend.at[w], ZL - 1, y_send.at[w, 0])
         wait_all(ysend.at[w], 2, y_send.at[w, 1])
         wait_all(ysend.at[w], 2, y_send.at[w, 2])
@@ -354,7 +397,12 @@
 
 
 def deliver(gt, gp, gwi, gwo, gt_out, gp_out, gwi_out, gwo_out, sem):
-    pairs = ((gwi, gwi_out), (gwo, gwo_out), (gt, gt_out), (gp, gp_out))
+    pairs = [(gt, gt_out), (gp, gp_out)]
+    for src, dst in ((gwi, gwi_out), (gwo, gwo_out)):
+        rows = src.shape[1] // 4
+        for part in range(8):
+            at = (part // 4, pl.ds(part % 4 * rows, rows))
+            pairs.append((src.at[at], dst.at[at]))
     copies = [pltpu.make_async_copy(src, dst, sem.at[k]) for k, (src, dst) in enumerate(pairs)]
     for copy in copies:
         copy.start()
@@ -390,7 +438,7 @@
         vmem((16, LANES), BF16), vmem((NZ, 16, LANES), BF16),
         vmem((16, LANES), BF16), vmem((T, 16, LANES), BF16),
         DMA((5,)), DMA((2,)), DMA((2,)), DMA((2,)), DMA((2,)), DMA((2,)),
-        DMA((2,)), DMA((2,)), DMA((2, 2)), DMA((2, 3)), DMA((2, 3)), DMA((2, 3)), DMA((2,)), DMA((2,)),
+        DMA((2,)), DMA((2,)), DMA((2,)), DMA((2, ZL + 2)), DMA((2, 3)), DMA((2, 3)), DMA((2,)), DMA((2,)),
         DMA, DMA, DMA, DMA, DMA, DMA,
     ]
     shapes = (
@@ -414,7 +462,7 @@
         out_shape=shapes,
         in_specs=[anywhere] * 4,
         out_specs=[in_hbm] * 4,
-        scratch_shapes=[DMA((4,))],
+        scratch_shapes=[DMA((18,))],
         compiler_params=pltpu.CompilerParams(vmem_limit_bytes=1024 * 1024),
     )(*results)
     return grad_tokens[None], grad_param.T, grad_win, grad_wout

time: 88.8 us -> 86.6 us (0.975)
  Pallas kernels: 88 us -> 85.9 us
    pallas_call x1, Pallas kernels: 85.8 us -> 83.5 us  [per_device(): pl.pallas_call(functools.partial(kernel, ZL, XY), out_shape=shapes, in_sp...]
where the time goes in v5:
time: 86.6 us
  Pallas kernels  85.9 us (99%)
    pallas_call x1, Pallas kernels, per_device(): pl.pallas_call(functools.partial(kernel, ZL, XY), out_shape=shapes, in_sp...  83.5 us
    pallas_call x1, Pallas kernels, per_device(): pl.pallas_call(deliver, out_shape=shapes, in_specs=[anywhere] * 4, out_sp...  2.4 us

profile of v5, /device:TPU:1, one launch (start us, length us, event | category | flops | bytes accessed | tf_op | source)
XLA Modules:
  0.0 86.6 jit_solution(15616480651171300708)
XLA Ops:
  0.6 83.5 %shard_map.84 = (bf16[256,1024]{1,0:T(8,128)(2,1)S(1)}, f32[64,1024]{1,0:T(8,128)S(1)}, bf16[2,1024,512]{2,1,0:T(8,128)(2,1)S(1)}, bf16[2,512,1024]{2,1,0:T(8,128)(2,1)S(1)}) custom-call(bf16[256,1024]{1,0:T(8,128)(2,1)} %bitcast.5, bf16[64,1024]{1,0:T(8,128)(2,1)} %bitcast.7, bf16[2,1024,512]{2,1,0:T(8,128)(2,1)} %wi_hbm.1, bf16[2,512,1024]{2,1,0:T(8,128)(2,1)} %wo_hbm.1, ...), custom_call_target="tpu_custom_call" | custom-call | tf_op jit(solution)/shard_map/pallas_call | solution.py:450
  84.2 2.4 %shard_map.85 = (bf16[256,1024]{1,0:T(8,128)(2,1)}, f32[64,1024]{1,0:T(8,128)}, bf16[2,1024,512]{2,1,0:T(8,128)(2,1)}, bf16[2,512,1024]{2,1,0:T(8,128)(2,1)}) custom-call(bf16[256,1024]{1,0:T(8,128)(2,1)S(1)} %get-tuple-element.12.gt, f32[64,1024]{1,0:T(8,128)S(1)} %get-tuple-element.13.gp, bf16[2,1024,512]{2,1,0:T(8,128)(2,1)S(1)} %get-tuple-element.14.gwi, ...), custom_call_target="tpu_custom_call" | custom-call | tf_op jit(solution)/shard_map/pallas_call | solution.py:460

commit v6 on v5

--- a/solution.py
+++ b/solution.py
@@ -264,8 +264,6 @@
 
     send_planes(0)
     send_planes(1)
-    for copy in loads[3:] + swap:
-        copy.wait()
     pass_on(0)
 
     rows = NZ * T
@@ -314,6 +312,8 @@
 
     pass_on(1)
     all_here(0)
+    for copy in loads[3:] + swap:
+        copy.wait()
     pre_part(0)
     pre_part(1)
     out_part(0)

time: 86.6 us -> 86.6 us (level)
  no operation moved by 1% of the time
where the time goes in v6:
time: 86.6 us
  Pallas kernels  85.9 us (99%)
    pallas_call x1, Pallas kernels, per_device(): pl.pallas_call(functools.partial(kernel, ZL, XY), out_shape=shapes, in_sp...  83.5 us
    pallas_call x1, Pallas kernels, per_device(): pl.pallas_call(deliver, out_shape=shapes, in_specs=[anywhere] * 4, out_sp...  2.4 us

profile of v6, /device:TPU:1, one launch (start us, length us, event | category | flops | bytes accessed | tf_op | source)
XLA Modules:
  0.0 86.6 jit_solution(10608054350221092843)
XLA Ops:
  0.6 83.5 %shard_map.84 = (bf16[256,1024]{1,0:T(8,128)(2,1)S(1)}, f32[64,1024]{1,0:T(8,128)S(1)}, bf16[2,1024,512]{2,1,0:T(8,128)(2,1)S(1)}, bf16[2,512,1024]{2,1,0:T(8,128)(2,1)S(1)}) custom-call(bf16[256,1024]{1,0:T(8,128)(2,1)} %bitcast.5, bf16[64,1024]{1,0:T(8,128)(2,1)} %bitcast.7, bf16[2,1024,512]{2,1,0:T(8,128)(2,1)} %wi_hbm.1, bf16[2,512,1024]{2,1,0:T(8,128)(2,1)} %wo_hbm.1, ...), custom_call_target="tpu_custom_call" | custom-call | tf_op jit(solution)/shard_map/pallas_call | solution.py:450
  84.2 2.4 %shard_map.85 = (bf16[256,1024]{1,0:T(8,128)(2,1)}, f32[64,1024]{1,0:T(8,128)}, bf16[2,1024,512]{2,1,0:T(8,128)(2,1)}, bf16[2,512,1024]{2,1,0:T(8,128)(2,1)}) custom-call(bf16[256,1024]{1,0:T(8,128)(2,1)S(1)} %get-tuple-element.12.gt, f32[64,1024]{1,0:T(8,128)S(1)} %get-tuple-element.13.gp, bf16[2,1024,512]{2,1,0:T(8,128)(2,1)S(1)} %get-tuple-element.14.gwi, ...), custom_call_target="tpu_custom_call" | custom-call | tf_op jit(solution)/shard_map/pallas_call | solution.py:460
